TPU v7x, 256 devices: a whole 4x4x8 slice. The times are simulated.
256 devices in a mesh: seq: 32 (over x, y, core), head: 8 (over z).
Axes of the slice: x: 4, y: 4, z: 8, core: 2. Of those that a mesh axis runs over, the one named last changes fastest.
Arguments:
- hidden_in: bfloat16 [16384, 2048], P('seq', 'head'), may hold values from -8 to 8
- proj_weight: bfloat16 [2048, 10240], P(None, 'head'), may hold values from -0.125 to 0.125
- beta_weight: bfloat16 [2048, 32], P(None, 'head'), may hold values from -1 to 1
- norm_gain: float32 [2048], P('head'), may hold values from 0.1 to 1.9
- out_weight: bfloat16 [2048, 2048], P('head'), may hold values from -0.125 to 0.125
- cotangent: bfloat16 [16384, 2048], P('seq', 'head'), may hold values from -6 to 6
Outputs:
- mixed_out: bfloat16 [16384, 2048], P('seq', 'head')
- grad_input: bfloat16 [16384, 2048], P('seq', 'head')
All inputs are finite; a program needn't handle non-finite values.
Results may differ from a plain program's by a relative error of at most 0.02.
Values may be sent and summed in bfloat16 or wider, within the bound.
A program may use at most 128 MiB of HBM per device.

v0:
```python
from functools import partial
import jax
import jax.numpy as jnp
from jax import lax
from jax.sharding import PartitionSpec as P

DK = 128
REFL = 2
HIGHEST = lax.Precision.HIGHEST


def passed_along(shard, axis, by):
    size = lax.axis_size(axis)
    pairs = [(i, i + by) for i in range(size) if 0 <= i + by < size]
    return lax.ppermute(shard, axis, pairs)


def product(left, right):
    return jnp.matmul(left, right, precision=HIGHEST)


def unit_rows(vectors):
    return vectors / jnp.sqrt(jnp.sum(vectors * vectors, axis=-1, keepdims=True) + 1e-06)


def solve_lower(matrix, target):
    return jax.scipy.linalg.solve_triangular(matrix, target, lower=True, unit_diagonal=True)


def prepare_head(projected, beta_logits, block_size):
    row_count = projected.shape[0]
    key_width = projected.shape[1] // (1 + 2 * REFL)
    blocks = row_count // block_size
    pair_span = block_size * REFL
    pieces = projected.reshape(row_count, 1 + 2 * REFL, key_width)
    queries = unit_rows(pieces[:, 0]).reshape(blocks, block_size, key_width)
    key_rows = unit_rows(pieces[:, 1 : 1 + REFL]).reshape(blocks, pair_span, key_width)
    values = pieces[:, 1 + REFL :].reshape(blocks, pair_span, key_width)
    strength = (2.0 * jax.nn.sigmoid(beta_logits)).reshape(blocks, pair_span, 1)
    strict_below = jnp.arange(pair_span)[:, None] > jnp.arange(pair_span)[None, :]
    key_gram = strength * product(key_rows, jnp.swapaxes(key_rows, 1, 2))
    lower_unit = jnp.where(strict_below, key_gram, 0.0) + jnp.eye(pair_span, dtype=jnp.float32)
    target = strength * jnp.concatenate([values, key_rows], axis=2)
    solved = jax.vmap(solve_lower)(lower_unit, target)
    return (queries, key_rows, solved[:, :, key_width:], solved[:, :, :key_width])


def compose_head(key_rows, shifts, updates):
    key_width = key_rows.shape[2]
    identity = jnp.eye(key_width, dtype=jnp.float32)
    trans_all = identity - product(jnp.swapaxes(key_rows, 1, 2), shifts)
    writes = product(jnp.swapaxes(key_rows, 1, 2), updates)

    def absorb(state_pair, block_pair):
        return (
            (
                product(block_pair[0], state_pair[0]),
                product(block_pair[0], state_pair[1]) + block_pair[1],
            ),
            None,
        )

    result, _ = lax.scan(absorb, (identity, jnp.zeros_like(identity)), (trans_all, writes))
    return result


def read_head(queries, key_rows, shifts, updates, start_state, gain_row):
    block_size = queries.shape[1]
    pair_span = key_rows.shape[1]
    visible = jnp.arange(pair_span)[None, :] <= REFL * jnp.arange(block_size)[:, None] + REFL - 1

    def advance(memory, block_items):
        query_blk, key_blk, shift_blk, update_blk = block_items
        corrected = update_blk - product(shift_blk, memory)
        scores = jnp.where(visible, product(query_blk, key_blk.T), 0.0)
        output = product(query_blk, memory) + product(scores, corrected)
        return (memory + product(key_blk.T, corrected), output)

    _, outputs = lax.scan(advance, start_state, (queries, key_rows, shifts, updates))
    outputs = outputs.reshape(-1, outputs.shape[2])
    inverse_rms = lax.rsqrt(jnp.mean(outputs * outputs, axis=-1, keepdims=True) + 1e-05)
    return outputs * inverse_rms * gain_row


def local(hidden_in, proj_weight, beta_weight, norm_gain, out_weight, cotangent):
    row_count = hidden_in.shape[0]
    block_size = min(64, row_count)
    head_count = norm_gain.shape[0] // DK
    head_width = proj_weight.shape[1] // head_count
    contract = (((1,), (1,)), ((), ()))
    hidden_part = lax.all_gather(hidden_in, "head", axis=1, tiled=True)
    cot_part = lax.all_gather(cotangent, "head", axis=1, tiled=True)
    projected = jnp.dot(hidden_part, proj_weight, preferred_element_type=jnp.float32)
    beta_logits = jnp.dot(hidden_part, beta_weight, preferred_element_type=jnp.float32)
    dnormed = lax.dot_general(cot_part, out_weight, contract, preferred_element_type=jnp.float32)
    projected, beta_logits, dnormed = (projected, beta_logits, dnormed)
    proj_heads = jnp.moveaxis(projected.reshape(row_count, head_count, head_width), 1, 0)
    logit_heads = jnp.moveaxis(beta_logits.reshape(row_count, head_count, REFL), 1, 0)
    gain_heads = norm_gain.reshape(head_count, DK)
    prepared, prep_pull = jax.vjp(
        jax.vmap(partial(prepare_head, block_size=block_size)), proj_heads, logit_heads
    )
    (transit, offset), compose_pull = jax.vjp(
        jax.vmap(compose_head), prepared[1], prepared[2], prepared[3]
    )
    turn_count = lax.axis_size("seq") - 1

    def forward_turn(turn_index, state_pair):
        incoming = passed_along(state_pair[1], "seq", 1)
        return (incoming, product(transit, incoming) + offset)

    start_state, _ = lax.fori_loop(0, turn_count, forward_turn, (jnp.zeros_like(offset), offset))

    def read_all(queries, key_rows, shifts, updates, memory):
        return jax.vmap(read_head)(queries, key_rows, shifts, updates, memory, gain_heads)

    normed, read_pull = jax.vjp(
        read_all, prepared[0], prepared[1], prepared[2], prepared[3], start_state
    )
    normed_rows = (
        jnp.moveaxis(normed, 0, 1).reshape(row_count, head_count * DK).astype(jnp.bfloat16)
    )
    mixed_terms = jnp.dot(normed_rows, out_weight, preferred_element_type=jnp.float32)
    mixed_out = lax.psum_scatter(
        mixed_terms.astype(jnp.bfloat16), "head", scatter_dimension=1, tiled=True
    )
    dnormed_heads = jnp.moveaxis(dnormed.reshape(row_count, head_count, DK), 1, 0)
    grad_query, grad_keys, grad_shifts, grad_updates, grad_start = read_pull(dnormed_heads)
    transit_back = jnp.swapaxes(transit, 1, 2)

    def backward_turn(turn_index, state_pair):
        arriving = passed_along(state_pair[1], "seq", -1)
        return (arriving, grad_start + product(transit_back, arriving))

    after_grad, _ = lax.fori_loop(
        0, turn_count, backward_turn, (jnp.zeros_like(grad_start), grad_start)
    )
    keys_extra, shifts_extra, updates_extra = compose_pull(
        (product(after_grad, jnp.swapaxes(start_state, 1, 2)), after_grad)
    )
    grad_proj, grad_logit = prep_pull(
        (
            grad_query,
            grad_keys + keys_extra,
            grad_shifts + shifts_extra,
            grad_updates + updates_extra,
        )
    )
    proj_back = (
        jnp.moveaxis(grad_proj, 0, 1)
        .reshape(row_count, head_count * head_width)
        .astype(jnp.bfloat16)
    )
    logit_back = (
        jnp.moveaxis(grad_logit, 0, 1).reshape(row_count, head_count * REFL).astype(jnp.bfloat16)
    )
    input_term = lax.dot_general(
        proj_back, proj_weight, contract, preferred_element_type=jnp.float32
    )
    input_term = input_term + lax.dot_general(
        logit_back, beta_weight, contract, preferred_element_type=jnp.float32
    )
    grad_input = lax.psum_scatter(
        input_term.astype(jnp.bfloat16), "head", scatter_dimension=1, tiled=True
    )
    return (mixed_out, grad_input)


def solution(mesh):
    placed = (
        P("seq", "head"),
        P(None, "head"),
        P(None, "head"),
        P("head"),
        P("head", None),
        P("seq", "head"),
    )
    return jax.shard_map(
        local,
        mesh=mesh,
        in_specs=placed,
        out_specs=(P("seq", "head"), P("seq", "head")),
        check_vma=False,
    )
```

profile of v0, /device:TPU:4, one launch (start us, length us, event | category | flops | bytes accessed | tf_op | source)
XLA Modules:
  0.0 1188.4 jit_solution(16306266539693993664)
XLA Ops:
  9.6 50.3 %all-gather.3.cloned.1.call-done = bf16[512,2048]{1,0:T(8,128)(2,1)} async-done(((bf16[512,256]{1,0:T(8,128)(2,1)}), bf16[512,2048]{1,0:T(8,128)(2,1)}) %all-gather.3.cloned.1.call-update) | async-done | bytes 2097168 | tf_op jit(solution)/shard_map/all_gather | solution.py:91
  81.3 159.1 %custom-call.10 = f32[2,8,1,128,128]{3,4,2,1,0:T(8,128)} custom-call(f32[2,8,1,128,128]{4,3,2,1,0:T(8,128)} %add_bitcast_fusion), custom_call_target="InvertDiagBlocksLowerTriangular" | custom-call | tf_op jit(solution)/shard_map/jvp(vmap(vmap(jit(_solve_triangular))))/triangular_solve | solution.py:27
  255.9 25.7 %while.113 = (s32[]{:T(128)}, f32[2,128,128]{2,1,0:T(8,128)S(1)}, f32[2,128,128]{2,1,0:T(8,128)S(1)}, f32[8,2,128,128]{3,2,1,0:T(8,128)}, f32[8,2,128,128]{3,2,1...) while((s32[]{:T(128)}, f32[2,128,128]{2,1,0:T(8,128)S(1)}, ...), condition=%wide.region_2.3_spmd.clone, body=%wide.region_1.0_spmd.clone.sunk | while | flops 100761600 | bytes 1967735 | solution.py:63
  282.2 280.3 %while.109 = (s32[]{:T(128)}, f32[2,128,128]{2,1,0:T(8,128)}, f32[2,128,128]{2,1,0:T(8,128)S(1)}, f32[2,128,128]{2,1,0:T(8,128)S(1)}, f32[2,128,128]{2,1,0:T(8,128)S(1)}, /*index=5*/s32[]{:T(128)}) while((s32[]{:T(128)}, f32[2,128,128]{2,1,0:T(8,128)}, f32[2,128,128]{2,1,0:T(8,128)S(1)}, f32[2,128,128]{2,1,0:T(8,128)S(1)}, ...), condition=%wide.region_4.5_spmd, body=%wide.region_3.4_spmd.sunk | while | flops 50364416 | bytes 1573001 | solution.py:112
  284.1 6.5 collective-permute-done
  293.2 6.5 collective-permute-done
  302.2 6.5 collective-permute-done
  311.3 6.5 collective-permute-done
  320.3 6.5 collective-permute-done
  338.4 6.5 collective-permute-done
  347.4 6.5 collective-permute-done
  365.5 6.5 collective-permute-done
  374.6 6.5 collective-permute-done
  392.6 6.5 collective-permute-done
  401.7 6.5 collective-permute-done
  419.8 6.5 collective-permute-done
  428.8 6.5 collective-permute-done
  437.8 6.5 collective-permute-done
  446.9 6.5 collective-permute-done
  455.9 6.5 collective-permute-done
  465.0 6.5 collective-permute-done
  483.0 6.5 collective-permute-done
  492.1 6.5 collective-permute-done
  510.2 6.5 collective-permute-done
  519.2 6.5 collective-permute-done
  537.3 6.5 collective-permute-done
  546.3 6.5 collective-permute-done
  570.5 50.5 %while.112 = (s32[]{:T(128)}, f32[2,128,128]{2,1,0:T(8,128)S(1)}, f32[8,2,64,128]{3,2,0,1:T(8,128)S(1)}, f32[8,2,128,128]{3,2,1,0:T(8,128)}, f32[8,2,128,128]{3,...) while((s32[]{:T(128)}, f32[2,128,128]{2,1,0:T(8,128)S(1)}, ...), condition=%wide.region_7.8_spmd.clone, body=%wide.region_6.7_spmd.clone.sunk | while | flops 176259072 | bytes 3156117 | solution.py:79
  633.6 117.7 %while.114 = (s32[]{:T(128)}, f32[2,128,128]{2,1,0:T(8,128)S(1)}, f32[8,2,64,128]{3,2,0,1:T(8,128)S(1)}, f32[8,2,128,128]{3,2,0,1:T(8,128)}, f32[8,2,128,128]{3,...) while((s32[]{:T(128)}, f32[2,128,128]{2,1,0:T(8,128)S(1)}, ...), condition=%wide.region_12.13_spmd.clone, body=%wide.region_11.12_spmd.clone.sunk | while | flops 352649216 | bytes 3883208 | solution.py:79
  752.1 276.2 %while.110 = (s32[]{:T(128)}, f32[2,128,128]{2,1,0:T(8,128)}, f32[2,128,128]{2,1,0:T(8,128)S(1)}, f32[2,128,128]{2,1,0:T(8,128)S(1)}, f32[2,128,128]{2,1,0:T(8,128)S(1)}, /*index=5*/s32[]{:T(128)}) while((s32[]{:T(128)}, f32[2,128,128]{2,1,0:T(8,128)}, f32[2,128,128]{2,1,0:T(8,128)S(1)}, f32[2,128,128]{2,1,0:T(8,128)S(1)}, ...), condition=%wide.region_14.15_spmd, body=%wide.region_13.14_spmd.sunk | while | flops 50364416 | bytes 1573001 | solution.py:135
  1030.9 47.4 %while.111 = (s32[]{:T(128)}, f32[2,128,128]{2,1,0:T(8,128)S(1)}, f32[2,128,128]{2,1,0:T(8,128)S(1)}, f32[8,2,128,128]{2,3,1,0:T(8,128)}, f32[8,2,128,128]{3,2,1...) while((s32[]{:T(128)}, f32[2,128,128]{2,1,0:T(8,128)S(1)}, ...), condition=%wide.region_16.17_spmd, body=%wide.region_15.16_spmd.sunk | while | flops 201359360 | bytes 2491529 | solution.py:63
  1137.2 44.4 %reduce-scatter.5.cloned.1.call-done = bf16[512,256]{1,0:T(8,128)(2,1)} async-done(((bf16[512,2048]{1,0:T(8,128)(2,1)}), bf16[512,256]{1,0:T(8,128)(2,1)}) %reduce-scatter.5.cloned.1.call-update) | async-done | bytes 262160 | tf_op jit(solution)/shard_map/reduce_scatter | solution.py:163
  (711 shorter events, 768.3 us)
Async XLA Ops:
  7.2 52.7 %all-gather.3.cloned.1.call-start = ((), (), s32[]{:S(2)}) async-start(), calls=%async_computation.2 | async-start | bytes 2359296 | tf_op jit(solution)/shard_map/all_gather | solution.py:91
  7.9 613.1 %all-gather.5.cloned.1.call-start = ((), (), s32[]{:S(2)}) async-start(), calls=%async_computation.4 | async-start | bytes 2359296 | tf_op jit(solution)/shard_map/all_gather | solution.py:92
  8.7 1128.5 %reduce-scatter.3.cloned.1.call-start = ((), (), s32[]{:S(2)}) async-start(), calls=%async_computation.3 | async-start | bytes 2359296 | tf_op jit(solution)/shard_map/reduce_scatter | solution.py:124
  757.2 8.4 collective-permute-start.1
  766.2 8.4 collective-permute-start.1
  775.3 8.4 collective-permute-start.1
  784.3 8.4 collective-permute-start.1
  793.3 8.4 collective-permute-start.1
  802.4 8.4 collective-permute-start.1
  811.4 8.4 collective-permute-start.1
  820.5 8.4 collective-permute-start.1
  829.5 8.4 collective-permute-start.1
  838.5 8.4 collective-permute-start.1
  847.6 8.4 collective-permute-start.1
  856.6 8.4 collective-permute-start.1
  865.7 8.4 collective-permute-start.1
  874.7 8.4 collective-permute-start.1
  883.7 8.4 collective-permute-start.1
  892.8 8.4 collective-permute-start.1
  901.8 8.4 collective-permute-start.1
  910.8 8.4 collective-permute-start.1
  919.9 8.4 collective-permute-start.1
  928.9 8.4 collective-permute-start.1
  938.0 8.4 collective-permute-start.1
  947.0 8.4 collective-permute-start.1
  956.0 8.4 collective-permute-start.1
  965.1 8.4 collective-permute-start.1
  974.1 8.4 collective-permute-start.1
  992.2 8.4 collective-permute-start.1
  1001.2 8.4 collective-permute-start.1
  1010.3 8.4 collective-permute-start.1
  1095.2 86.4 %reduce-scatter.5.cloned.1.call-start = ((), (), s32[]{:S(2)}) async-start(), calls=%async_computation.5 | async-start | bytes 2359296 | tf_op jit(solution)/shard_map/reduce_scatter | solution.py:163
  (138 other events, 2319.2 us)
Sparse Core Ops, SparseCore 0:
  9.7 50.0 all-gather.2
  61.6 47.7 all-gather.4
  1095.3 41.8 reduce-scatter.2
  1140.2 41.3 reduce-scatter.4
where the time goes:
time: 1200 us; the launch traced here: 1190 us
  waiting for transfers between devices  377 us (31%)
  matrix products  306 us (26%)
  starting transfers between devices  238 us (20%)
  other arithmetic  181 us (15%)
  local copies, waits for them, and re-layouts  68.9 us (6%)
  between operations  14.7 us (1%)
    ppermute x62, waiting for transfers between devices, passed_along(): return lax.ppermute(shard, axis, pairs)  278 us
    dot_general x240, matrix products, product(): return jnp.matmul(left, right, precision=HIGHEST)  271 us
    ppermute x62, starting transfers between devices, passed_along(): return lax.ppermute(shard, axis, pairs)  237 us
    another operation x3, other arithmetic, solve_lower(): jax.scipy.linalg.solve_triangular(matrix, target, lower=True, unit_diagon...  162 us
    all_gather x1, waiting for transfers between devices, local(): hidden_part = lax.all_gather(hidden_in, 'head', axis=1, tiled=True)  50.3 us
    reduce_scatter x1, waiting for transfers between devices, local(): lax.psum_scatter(input_term.astype(jnp.bfloat16), 'head', scatter_dimensi...  44.4 us
  transfers between devices with their start and end apart: 66, of which 65 were waited for; matrix products, arithmetic and copies ran while one was open for 27% of the time, Pallas kernels for 0%

commit v1 on v0

--- a/solution.py
+++ b/solution.py
@@ -3,6 +3,7 @@
 import jax.numpy as jnp
 from jax import lax
 from jax.sharding import PartitionSpec as P
+from jax.lax import all_gather
 
 DK = 128
 REFL = 2
@@ -88,8 +89,11 @@
     head_count = norm_gain.shape[0] // DK
     head_width = proj_weight.shape[1] // head_count
     contract = (((1,), (1,)), ((), ()))
-    hidden_part = lax.all_gather(hidden_in, "head", axis=1, tiled=True)
-    cot_part = lax.all_gather(cotangent, "head", axis=1, tiled=True)
+    hidden_part, cot_part = jnp.split(
+        all_gather(jnp.concatenate([hidden_in, cotangent], 0), "head", axis=1, tiled=True),
+        [hidden_in.shape[0]],
+        0,
+    )
     projected = jnp.dot(hidden_part, proj_weight, preferred_element_type=jnp.float32)
     beta_logits = jnp.dot(hidden_part, beta_weight, preferred_element_type=jnp.float32)
     dnormed = lax.dot_general(cot_part, out_weight, contract, preferred_element_type=jnp.float32)

time: 1200 us -> 1290 us (1.075)
  waiting for transfers between devices: 377 us -> 435 us
  matrix products: 306 us -> 341 us
    reduce_scatter x1, waiting for transfers between devices: 2.99 us -> 44.1 us  [local(): lax.psum_scatter(mixed_terms.astype(jnp.bfloat16), 'head', scatter_dimens...]
    dot_general x240, matrix products: 271 us -> 308 us  [product(): return jnp.matmul(left, right, precision=HIGHEST)]
    all_gather x2 -> x1, waiting for transfers between devices: 50.3 us -> 64.9 us  [local(): all_gather(jnp.concatenate([hidden_in, cotangent], 0), 'head', axis=1, ti...]
  transfers between devices with their start and end apart: 66 -> 65, of which waited for: 65 -> 65; matrix products, arithmetic and copies ran while one was open for 27% -> 0% of each run, Pallas kernels for 0% -> 0%
where the time goes in v1:
time: 1290 us; the launch traced here: 1280 us
  waiting for transfers between devices  435 us (34%)
  matrix products  341 us (26%)
  starting transfers between devices  238 us (18%)
  other arithmetic  186 us (14%)
  local copies, waits for them, and re-layouts  58.3 us (5%)
  between operations  14.7 us (1%)
    dot_general x240, matrix products, product(): return jnp.matmul(left, right, precision=HIGHEST)  308 us
    ppermute x62, waiting for transfers between devices, passed_along(): return lax.ppermute(shard, axis, pairs)  288 us
    ppermute x62, starting transfers between devices, passed_along(): return lax.ppermute(shard, axis, pairs)  237 us
    another operation x3, other arithmetic, solve_lower(): jax.scipy.linalg.solve_triangular(matrix, target, lower=True, unit_diagon...  161 us
    all_gather x1, waiting for transfers between devices, local(): all_gather(jnp.concatenate([hidden_in, cotangent], 0), 'head', axis=1, ti...  64.9 us
    reduce_scatter x1, waiting for transfers between devices, local(): lax.psum_scatter(mixed_terms.astype(jnp.bfloat16), 'head', scatter_dimens...  44.1 us
    reduce_scatter x1, waiting for transfers between devices, local(): lax.psum_scatter(input_term.astype(jnp.bfloat16), 'head', scatter_dimensi...  38.4 us
  transfers between devices with their start and end apart: 65, of which 65 were waited for; matrix products, arithmetic and copies ran while one was open for 0% of the time, Pallas kernels for 0%

profile of v1, /device:TPU:4, one launch (start us, length us, event | category | flops | bytes accessed | tf_op | source)
XLA Modules:
  0.0 1275.5 jit_solution(1442833844091506605)
XLA Ops:
  10.1 64.9 %all-gather.2.cloned.1.call-done = bf16[1024,2048]{1,0:T(8,128)(2,1)} async-done(((bf16[1024,256]{1,0:T(8,128)(2,1)}), bf16[1024,2048]{1,0:T(8,128)(2,1)}) %all-gather.2.cloned.1.call-update) | async-done | bytes 4194320 | tf_op jit(solution)/shard_map/all_gather | solution.py:93
  95.4 158.6 %custom-call.10 = f32[2,8,1,128,128]{3,4,2,1,0:T(8,128)} custom-call(f32[2,8,1,128,128]{4,3,2,1,0:T(8,128)} %add_bitcast_fusion), custom_call_target="InvertDiagBlocksLowerTriangular" | custom-call | tf_op jit(solution)/shard_map/jvp(vmap(vmap(jit(_solve_triangular))))/triangular_solve | solution.py:28
  272.8 18.0 %while.113 = (s32[]{:T(128)}, f32[2,128,128]{2,1,0:T(8,128)S(1)}, f32[2,128,128]{2,1,0:T(8,128)S(1)}, f32[8,2,128,128]{3,2,1,0:T(8,128)}, f32[8,2,128,128]{3,2,1...) while((s32[]{:T(128)}, f32[2,128,128]{2,1,0:T(8,128)S(1)}, ...), condition=%wide.region_2.3_spmd.clone, body=%wide.region_1.0_spmd.clone.sunk | while | flops 100761600 | bytes 1967724 | solution.py:64
  292.2 326.4 %while.109 = (s32[]{:T(128)}, f32[2,128,128]{2,1,0:T(8,128)}, f32[2,128,128]{2,1,0:T(8,128)}, f32[2,128,128]{2,1,0:T(8,128)S(1)}, f32[2,128,128]{2,1,0:T(8,128)S(1)}, /*index=5*/s32[]{:T(128)}) while((s32[]{:T(128)}, f32[2,128,128]{2,1,0:T(8,128)}, f32[2,128,128]{2,1,0:T(8,128)}, f32[2,128,128]{2,1,0:T(8,128)S(1)}, ...), condition=%wide.region_4.5_spmd, body=%wide.region_3.4_spmd.sunk | while | flops 50364416 | bytes 1048685 | solution.py:116
  294.1 6.8 collective-permute-done
  304.6 6.8 collective-permute-done
  315.2 6.8 collective-permute-done
  325.7 6.8 collective-permute-done
  336.2 6.8 collective-permute-done
  346.8 6.8 collective-permute-done
  357.3 6.8 collective-permute-done
  367.8 6.8 collective-permute-done
  378.4 6.8 collective-permute-done
  388.9 6.8 collective-permute-done
  399.4 6.8 collective-permute-done
  409.9 6.8 collective-permute-done
  420.5 6.8 collective-permute-done
  431.0 6.8 collective-permute-done
  441.5 6.8 collective-permute-done
  452.1 6.8 collective-permute-done
  462.6 6.8 collective-permute-done
  473.1 6.8 collective-permute-done
  483.7 6.8 collective-permute-done
  494.2 6.8 collective-permute-done
  504.7 6.8 collective-permute-done
  589.0 6.8 collective-permute-done
  629.7 50.6 %while.112 = (s32[]{:T(128)}, f32[2,128,128]{2,1,0:T(8,128)S(1)}, f32[8,2,64,128]{3,2,0,1:T(8,128)S(1)}, f32[8,2,128,128]{3,2,1,0:T(8,128)}, f32[8,2,128,128]{3,...) while((s32[]{:T(128)}, f32[2,128,128]{2,1,0:T(8,128)S(1)}, ...), condition=%wide.region_7.8_spmd.clone, body=%wide.region_6.7_spmd.clone.sunk | while | flops 176259072 | bytes 3157125 | solution.py:80
  691.0 117.9 %while.114 = (s32[]{:T(128)}, f32[2,128,128]{2,1,0:T(8,128)S(1)}, f32[8,2,64,128]{3,2,0,1:T(8,128)S(1)}, f32[8,2,128,128]{3,2,0,1:T(8,128)}, f32[8,2,128,128]{3,...) while((s32[]{:T(128)}, f32[2,128,128]{2,1,0:T(8,128)S(1)}, ...), condition=%wide.region_12.13_spmd.clone, body=%wide.region_11.12_spmd.clone.sunk | while | flops 352649216 | bytes 3883200 | solution.py:80
  809.7 276.3 %while.110 = (s32[]{:T(128)}, f32[2,128,128]{2,1,0:T(8,128)}, f32[2,128,128]{2,1,0:T(8,128)S(1)}, f32[2,128,128]{2,1,0:T(8,128)S(1)}, f32[2,128,128]{2,1,0:T(8,128)S(1)}, /*index=5*/s32[]{:T(128)}) while((s32[]{:T(128)}, f32[2,128,128]{2,1,0:T(8,128)}, f32[2,128,128]{2,1,0:T(8,128)S(1)}, f32[2,128,128]{2,1,0:T(8,128)S(1)}, ...), condition=%wide.region_14.15_spmd, body=%wide.region_13.14_spmd.sunk | while | flops 50364416 | bytes 1573001 | solution.py:139
  1088.5 47.7 %while.111 = (s32[]{:T(128)}, f32[2,128,128]{2,1,0:T(8,128)S(1)}, f32[2,128,128]{2,1,0:T(8,128)S(1)}, f32[8,2,128,128]{2,3,1,0:T(8,128)}, f32[8,2,128,128]{3,2,1...) while((s32[]{:T(128)}, f32[2,128,128]{2,1,0:T(8,128)S(1)}, ...), condition=%wide.region_16.17_spmd, body=%wide.region_15.16_spmd.sunk | while | flops 201359360 | bytes 2491521 | solution.py:64
  1186.3 38.4 %reduce-scatter.5.cloned.1.call-done = bf16[512,256]{1,0:T(8,128)(2,1)} async-done(((bf16[512,2048]{1,0:T(8,128)(2,1)}), bf16[512,256]{1,0:T(8,128)(2,1)}) %reduce-scatter.5.cloned.1.call-update) | async-done | bytes 262160 | tf_op jit(solution)/shard_map/reduce_scatter | solution.py:167
  1224.6 44.1 %reduce-scatter.3.cloned.1.call-done = bf16[512,256]{1,0:T(8,128)(2,1)} async-done(((bf16[512,2048]{1,0:T(8,128)(2,1)}), bf16[512,256]{1,0:T(8,128)(2,1)}) %reduce-scatter.3.cloned.1.call-update) | async-done | bytes 262160 | tf_op jit(solution)/shard_map/reduce_scatter | solution.py:128
  (641 shorter events, 802.9 us)
Async XLA Ops:
  7.2 67.8 %all-gather.2.cloned.1.call-start = ((), (), s32[]{:S(2)}) async-start(), calls=%async_computation.2 | async-start | bytes 4718592 | tf_op jit(solution)/shard_map/all_gather | solution.py:93
  9.2 1215.4 %reduce-scatter.5.cloned.1.call-start = ((), (), s32[]{:S(2)}) async-start(), calls=%async_computation.4 | async-start | bytes 2359296 | tf_op jit(solution)/shard_map/reduce_scatter | solution.py:167
  292.2 8.7 collective-permute-start
  302.7 8.7 collective-permute-start
  313.3 8.7 collective-permute-start
  323.8 8.7 collective-permute-start
  334.3 8.7 collective-permute-start
  344.8 8.7 collective-permute-start
  355.4 8.7 collective-permute-start
  365.9 8.7 collective-permute-start
  376.4 8.7 collective-permute-start
  387.0 8.7 collective-permute-start
  397.5 8.7 collective-permute-start
  408.0 8.7 collective-permute-start
  418.6 8.7 collective-permute-start
  429.1 8.7 collective-permute-start
  439.6 8.7 collective-permute-start
  450.2 8.7 collective-permute-start
  460.7 8.7 collective-permute-start
  471.2 8.7 collective-permute-start
  481.7 8.7 collective-permute-start
  492.3 8.7 collective-permute-start
  502.8 8.7 collective-permute-start
  523.9 8.7 collective-permute-start
  534.4 8.7 collective-permute-start
  544.9 8.7 collective-permute-start
  555.5 8.7 collective-permute-start
  566.0 8.7 collective-permute-start
  576.5 8.7 collective-permute-start
  587.0 8.7 collective-permute-start
  597.6 8.7 collective-permute-start
  1183.1 85.6 %reduce-scatter.3.cloned.1.call-start = ((), (), s32[]{:S(2)}) async-start(), calls=%async_computation.3 | async-start | bytes 2359296 | tf_op jit(solution)/shard_map/reduce_scatter | solution.py:128
  (103 other events, 1656.4 us)
Sparse Core Ops, SparseCore 0:
  9.7 65.2 all-gather.1
  1183.2 41.3 reduce-scatter.4
  1227.8 40.9 reduce-scatter.2
